TPU v7x, 512 devices: a whole 4x8x8 slice. The times are simulated.
512 devices in a mesh: wide: 64 (over z_lo, y, core), narrow: 8 (over x, z_hi).
Axes of the slice: x: 4, y: 8, z: 8 (z_hi: 2, z_lo: 4; z = z_hi * 4 + z_lo), core: 2. Of those that a mesh axis runs over, the one named last changes fastest.
Arguments:
- features: bfloat16 [16, 1024, 2, 1024], P(None, 'wide', None, 'narrow'), may hold values from -6 to 6
- cotangent: bfloat16 [16, 1024, 2, 1024], P(None, 'wide', None, 'narrow'), may hold values from -6 to 6
- coarse_weight: bfloat16 [32, 16, 3, 3, 3], replicated, may hold values from -0.3125 to 0.3125
- fine_weight: bfloat16 [16, 48, 3, 3, 3], replicated, may hold values from -0.15625 to 0.15625
Outputs:
- output: bfloat16 [16, 1024, 2, 1024], P(None, 'wide', None, 'narrow')
- grad_features: bfloat16 [16, 1024, 2, 1024], P(None, 'wide', None, 'narrow')
- grad_fine: float32 [16, 48, 3, 3, 3], replicated
- grad_coarse: float32 [32, 16, 3, 3, 3], replicated
All inputs are finite; a program needn't handle non-finite values.
Results may differ from a plain program's by a relative error of at most 0.012.
Values may be sent and summed in bfloat16 or wider, within the bound.
A program may use at most 64 MiB of HBM per device.

v0:
```python
import math
import jax
import jax.numpy as jnp
from jax import lax
from jax.sharding import PartitionSpec as P


def extended_2(array, sides, width):
    for axis, dim in sides:
        count, length = (lax.axis_size(axis), array.shape[dim])
        up = [(i, (i + 1) % count) for i in range(count - 1)]
        down = [(j, i) for i, j in up]
        last = lax.slice_in_dim(array, length - width, length, axis=dim)
        first = lax.slice_in_dim(array, 0, width, axis=dim)
        before = lax.ppermute(last, axis, up)
        after = lax.ppermute(first, axis, down)
        array = jnp.concatenate([before, array, after], axis=dim)
    return array


def shortened(array):
    return jax.tree.map(lambda a: a.astype(jnp.bfloat16) if a.dtype == jnp.float32 else a, array)


def correlate(padded, kernel):
    result = lax.conv_general_dilated(
        padded[None],
        kernel,
        (1, 1, 1),
        "VALID",
        dimension_numbers=("NCHWD", "OIHWD", "NCHWD"),
        preferred_element_type=jnp.float32,
    )
    return result[0]


def weight_grad(padded, grad):
    result = lax.conv_general_dilated(
        padded[:, None],
        grad[:, None],
        (1, 1, 1),
        "VALID",
        dimension_numbers=("NCHWD", "OIHWD", "NCHWD"),
        preferred_element_type=jnp.float32,
    )
    return jnp.transpose(result, (1, 0, 2, 3, 4))


def flipped(kernel):
    return jnp.transpose(kernel[:, :, ::-1, ::-1, ::-1], (1, 0, 2, 3, 4))


def pool_sum(field):
    chans, rows, planes, cols = field.shape
    return field.reshape(chans, rows // 2, 2, planes // 2, 2, cols // 2, 2).sum(axis=(2, 4, 6))


def upsample(field):
    chans, rows, planes, cols = field.shape
    spread = jnp.broadcast_to(
        field[:, :, None, :, None, :, None], (chans, rows, 2, planes, 2, cols, 2)
    )
    return spread.reshape(chans, 2 * rows, 2 * planes, 2 * cols)


def silu_slope(value):
    sig = jax.nn.sigmoid(value)
    return sig * (1.0 + value * (1.0 - sig))


def fine_padded(field):
    extended = extended_2(field, (("wide", 1), ("narrow", 3)), 1)
    return jnp.pad(extended, ((0, 0), (0, 0), (1, 1), (0, 0)))


def coarse_padded(field):
    extended = extended_2(field, ((("wide", "narrow"), 1),), 1)
    return jnp.pad(extended, ((0, 0), (0, 0), (1, 1), (1, 1)))


def into_coarse(field):
    return jax.tree.map(
        lambda part, own: part.astype(own.dtype),
        lax.all_to_all(shortened(field), "narrow", split_axis=1, concat_axis=3, tiled=True),
        field,
    )


def into_fine(field):
    return jax.tree.map(
        lambda part, own: part.astype(own.dtype),
        lax.all_to_all(shortened(field), "narrow", split_axis=3, concat_axis=1, tiled=True),
        field,
    )


def shards(features, cotangent, coarse_weight, fine_weight):
    channels = features.shape[0]
    pooled = (pool_sum(features.astype(jnp.float32)) / 8.0).astype(jnp.bfloat16)
    coarse_ext = coarse_padded(into_coarse(pooled))
    coarse_pre = correlate(coarse_ext, coarse_weight)
    coarse_act = jax.nn.silu(coarse_pre).astype(jnp.bfloat16)
    upsampled = upsample(into_fine(coarse_act))
    joined_ext = fine_padded(jnp.concatenate([features, upsampled], 0))
    cotangent_ext = fine_padded(cotangent)
    output = correlate(joined_ext, fine_weight).astype(jnp.bfloat16)
    local_fine = weight_grad(joined_ext, cotangent)
    grad_joined = correlate(cotangent_ext, flipped(fine_weight))
    grad_act = into_coarse(pool_sum(grad_joined[channels:]).astype(jnp.bfloat16))
    grad_pre = (grad_act.astype(jnp.float32) * silu_slope(coarse_pre)).astype(jnp.bfloat16)
    local_coarse = weight_grad(coarse_ext, grad_pre)
    grad_pooled = correlate(coarse_padded(grad_pre), flipped(coarse_weight)).astype(jnp.bfloat16)
    grad_features = (
        grad_joined[:channels] + upsample(into_fine(grad_pooled)).astype(jnp.float32) / 8.0
    ).astype(jnp.bfloat16)
    fine_total, coarse_total = lax.psum((local_fine, local_coarse), ("wide", "narrow"))
    all_cells = (
        features.shape[1]
        * features.shape[2]
        * features.shape[3]
        * lax.axis_size("wide")
        * lax.axis_size("narrow")
    )
    return (
        output,
        grad_features,
        fine_total / math.sqrt(all_cells),
        coarse_total / math.sqrt(all_cells // 8),
    )


def solution(mesh):
    placed = (P(None, "wide", None, "narrow"), P(None, "wide", None, "narrow"), P(), P())
    return jax.shard_map(
        shards,
        mesh=mesh,
        in_specs=placed,
        out_specs=(P(None, "wide", None, "narrow"), P(None, "wide", None, "narrow"), P(), P()),
        check_vma=False,
    )
```

profile of v0, /device:TPU:1, one launch (start us, length us, event | category | flops | bytes accessed | tf_op | source)
XLA Modules:
  0.0 639.0 jit_solution(16950988302908629010)
XLA Ops:
  7.2 0.8 fusion.97
  8.0 4.6 collective-permute-start.6
  12.6 5.5 collective-permute-start.7
  18.1 1.3 convert_reduce_fusion
  19.7 0.9 reduce_sum.25
  21.0 1.3 collective-permute-start.9
  22.3 8.1 %collective-permute-start.8 = (bf16[16,18,2,1]{3,2,1,0:T(2,128)(2,1)S(1)}, bf16[16,18,2,1]{3,2,1,0:T(2,128)(2,1)S(1)}, u32[]{:S(2)}, u32[]{:S(2)}) collective-permute-start(bf16[16,18,2,1]{3,2,1,0:T(2,128)(2,1)S(1)} %get-tuple-element.36), channel_id=1, source_target_pairs={{0,1},{1,2},{2,3},{3,4},{4,5},{5,6},{6,7},{8,9},{9,10},{10,11},{11... | collective-permute-start | bytes 3464 | tf_op jit(solution)/shard_map/ppermute | solution.py:15
  30.6 0.7 reshape.289
  31.3 10.0 %all-to-all-start = ((bf16[8,2,512]{2,1,0:T(2,128)(2,1)}), bf16[8,2,512]{2,1,0:T(2,128)(2,1)S(1)}, u32[]{:S(2)}, u32[]{:S(2)}) async-start(bf16[8,2,512]{2,1,0:T(2,128)(2,1)} %reshape.289), calls=%async_computation | async-start | bytes 32768 | tf_op jit(solution)/shard_map/all_to_all | solution.py:84
  41.3 3.8 copy.231
  45.1 1.3 fusion.54
  46.7 1.8 reshape.286
  48.5 5.1 copy.219
  53.6 1.0 slice.64
  54.7 5.0 fusion.26
  60.4 2.0 copy.221
  62.6 8.5 %collective-permute-start.1 = (bf16[16,1,1,512]{3,0,2,1:T(8,128)(2,1)S(1)}, bf16[16,1,1,512]{3,0,2,1:T(8,128)(2,1)S(1)}, u32[]{:S(2)}, u32[]{:S(2)}) collective-permute-start(bf16[16,1,1,512]{3,0,2,1:T(8,128)(2,1)S(1)} %all_to_all.11), channel_id=1, source_target_pairs={{1,0},{2,1},{3,2},{4,3},{5,4},{6,5},{7,6},{8,7},{9,8},{10,9},{11,1... | collective-permute-start | bytes 49160 | tf_op jit(solution)/shard_map/ppermute | solution.py:16
  71.1 2.1 collective-permute-start
  73.2 1.9 slice_reduce_fusion
  75.1 1.8 reduce_sum.37
  76.9 1.0 copy.222
  77.9 0.7 reshape.287
  78.6 10.8 %all-to-all-start.2 = ((bf16[8,2,1024]{2,1,0:T(2,128)(2,1)}), bf16[8,2,1024]{2,1,0:T(2,128)(2,1)S(1)}, u32[]{:S(2)}, u32[]{:S(2)}) async-start(bf16[8,2,1024]{2,1,0:T(2,128)(2,1)} %reshape.287), calls=%async_computation.2 | async-start | bytes 65536 | tf_op jit(solution)/shard_map/all_to_all | solution.py:84
  89.4 2.8 copy.220
  92.2 2.8 reshape.252
  95.0 0.8 fusion.98
  96.1 0.8 copy.204
  97.0 1.2 fusion.46
  98.2 0.8 fusion.99
  99.3 2.0 copy.233
  101.6 8.2 %collective-permute-start.11 = (bf16[32,1,1,512]{3,0,2,1:T(8,128)(2,1)S(1)}, bf16[32,1,1,512]{3,0,2,1:T(8,128)(2,1)S(1)}, u32[]{:S(2)}, u32[]{:S(2)}) collective-permute-start(bf16[32,1,1,512]{3,0,2,1:T(8,128)(2,1)S(1)} %get-tuple-element.40), channel_id=1, source_target_pairs={{1,0},{2,1},{3,2},{4,3},{5,4},{6,5},{7,6},{8,7},{9,8},{10,9},{11,1... | collective-permute-start | bytes 98312 | tf_op jit(solution)/shard_map/ppermute | solution.py:16
  109.7 1.9 collective-permute-start.10
  112.4 1.5 reduce.8
  113.9 0.8 reshape.291
  114.7 11.2 %all-to-all-start.1 = ((bf16[8,2,1024]{2,1,0:T(2,128)(2,1)}), bf16[8,2,1024]{2,1,0:T(2,128)(2,1)S(1)}, u32[]{:S(2)}, u32[]{:S(2)}) async-start(bf16[8,2,1024]{2,1,0:T(2,128)(2,1)} %reshape.291), calls=%async_computation.1 | async-start | bytes 65536 | tf_op jit(solution)/shard_map/all_to_all | solution.py:92
  126.1 5.7 fusion.101
  131.8 105.8 %psum.15 = f32[32,16,3,3,3]{0,1,4,3,2:T(8,128)S(1)} all-reduce(f32[32,16,3,3,3]{0,1,4,3,2:T(8,128)S(1)} %fusion.101), channel_id=1, replica_groups=mesh['wide'=64,'narrow'=8] {'wide','narrow'}, use_global_device_ids=true, to_apply=%region_5.6 | all-reduce | flops 13824 | bytes 110592 | tf_op jit(solution)/shard_map/psum | solution.py:116
  237.6 0.7 broadcast_multiply_fusion
  239.0 1.7 copy.225
  240.8 1.1 fusion.33
  242.3 1.5 reduce.9
  243.8 0.8 reshape.293
  244.6 3.3 all-to-all-start.3
  248.9 2.9 collective-permute-start.3
  251.8 2.6 collective-permute-start.2
  254.4 2.4 all-to-all-done.3
  258.3 1.3 collective-permute-start.5
  259.6 8.3 %collective-permute-start.4 = (bf16[48,18,2,1]{3,0,2,1:T(8,128)(2,1)S(1)}, bf16[48,18,2,1]{3,0,2,1:T(8,128)(2,1)S(1)}, u32[]{:S(2)}, u32[]{:S(2)}) collective-permute-start(bf16[48,18,2,1]{3,0,2,1:T(8,128)(2,1)S(1)} %get-tuple-element.32), channel_id=1, source_target_pairs={{0,1},{1,2},{2,3},{3,4},{4,5},{5,6},{6,7},{8,9},{9,10},{10,11},{11... | collective-permute-start | bytes 10376 | tf_op jit(solution)/shard_map/ppermute | solution.py:15
  268.0 0.8 copy.236
  268.7 5.5 collective-permute-done.5
  274.2 0.9 collective-permute-done.4
  275.2 0.8 copy-done.1
  275.9 2.0 fusion.111
  277.9 4.9 copy.240
  282.8 1.3 pad.22.clone
  284.5 6.5 %fusion.9 = bf16[16,2,8,17,16]{4,2,3,1,0:T(8,128)(2,1)} fusion(bf16[16,48,3,3,3]{1,0,4,3,2:T(8,128)(2,1)S(1)} %copy-done, bf16[48,18,4,1,7,2]{0,4,5,2,1,3:T(8,128)(2,1)S(1)} %slice.60, bf16[48,18,4,1,8,17]{0,4,5,2,1,3:T(8,128)(2,1)S(1)} %copy.213), kind=kOutput, calls=%fused_computation.12 | convolution fusion | flops 183638016 | bytes 1217536 | tf_op jit(solution)/shard_map/conv_general_dilated | solution.py:26
  291.0 2.7 copy.214
  294.4 0.7 reshape.245
  295.1 1.1 fusion.110
  296.2 8.8 %copy.230 = bf16[48,1,18,4,130]{0,1,4,3,2:T(2,128)(2,1)} copy(bf16[48,1,18,4,130]{4,0,3,2,1:T(8,128)(2,1)S(1)} %fusion.110) | data formatting | bytes 1797120 | tf_op jit(solution)/shard_map/broadcast_in_dim | solution.py:39
  305.0 31.3 %fusion.100 = f32[16,48,3,3,3]{1,0,4,3,2:T(8,128)} fusion(bf16[48,1,18,4,130]{0,1,4,3,2:T(2,128)(2,1)} %copy.230, bf16[16,1,16,2,128]{0,1,4,3,2:T(2,128)(2,1)} %copy.231), kind=kOutput, calls=%fused_computation.139 | convolution fusion | flops 169869312 | bytes 1112576 | tf_op jit(solution)/shard_map/transpose | solution.py:46
  336.3 0.8 copy.235
  337.1 293.2 %all-reduce.6.cloned.1.call-done = f32[16,48,3,3,3]{1,0,4,3,2:T(8,128)} async-done(((f32[16,48,3,3,3]{1,0,4,3,2:T(8,128)}), f32[16,48,3,3,3]{1,0,4,3,2:T(8,128)}) %all-reduce.6.cloned.1.call-update) | async-done | bytes 82960 | tf_op jit(solution)/shard_map/psum | solution.py:116
  630.3 1.6 broadcast_multiply_fusion.1
  (91 shorter events, 8.5 us)
Async XLA Ops:
  7.2 47.5 %copy-start = (bf16[16,48,3,3,3]{1,0,4,3,2:T(8,128)(2,1)S(1)}, bf16[16,48,3,3,3]{1,0,4,3,2:T(8,128)(2,1)}, u32[]{:S(2)}) copy-start(bf16[16,48,3,3,3]{1,0,4,3,2:T(8,128)(2,1)} %param.7) | copy-start | bytes 124420
  7.2 13.4 %copy-start.4 = (bf16[16,16,2,128]{3,2,1,0:T(2,128)(2,1)S(1)}, bf16[16,16,2,128]{3,2,1,0:T(2,128)(2,1)}, u32[]{:S(2)}) copy-start(bf16[16,16,2,128]{3,2,1,0:T(2,128)(2,1)} %param.5) | copy-start | bytes 393220
  7.2 34.1 %copy-start.5 = (bf16[16,16,2,128]{3,2,1,0:T(2,128)(2,1)S(1)}, bf16[16,16,2,128]{3,2,1,0:T(2,128)(2,1)}, u32[]{:S(2)}) copy-start(bf16[16,16,2,128]{3,2,1,0:T(2,128)(2,1)} %param.4) | copy-start | bytes 393220
  8.0 12.6 %collective-permute-start.6 = (bf16[16,1,2,128]{3,2,1,0:T(2,128)(2,1)S(1)}, bf16[16,1,2,128]{3,2,1,0:T(2,128)(2,1)S(1)}, u32[]{:S(2)}, u32[]{:S(2)}) collective-permute-start(bf16[16,1,2,128]{3,2,1,0:T(2,128)(2,1)S(1)} %get-tuple-element.39), channel_id=1, source_target_pairs={{0,8},{8,16},{16,24},{24,32},{32,40},{40,48},{48,56},{56,64},{64,7... | collective-permute-start | bytes 24584 | tf_op jit(solution)/shard_map/ppermute | solution.py:15
  12.6 8.1 %collective-permute-start.7 = (bf16[16,1,2,128]{3,2,1,0:T(2,128)(2,1)S(1)}, bf16[16,1,2,128]{3,2,1,0:T(2,128)(2,1)S(1)}, u32[]{:S(2)}, u32[]{:S(2)}) collective-permute-start(bf16[16,1,2,128]{3,2,1,0:T(2,128)(2,1)S(1)} %get-tuple-element.38), channel_id=1, source_target_pairs={{8,0},{16,8},{24,16},{32,24},{40,32},{48,40},{56,48},{64,56},{72,6... | collective-permute-start | bytes 24584 | tf_op jit(solution)/shard_map/ppermute | solution.py:16
  21.0 24.1 %collective-permute-start.9 = (bf16[16,18,2,1]{3,2,1,0:T(2,128)(2,1)S(1)}, bf16[16,18,2,1]{3,2,1,0:T(2,128)(2,1)S(1)}, u32[]{:S(2)}, u32[]{:S(2)}) collective-permute-start(bf16[16,18,2,1]{3,2,1,0:T(2,128)(2,1)S(1)} %get-tuple-element.37), channel_id=1, source_target_pairs={{1,0},{2,1},{3,2},{4,3},{5,4},{6,5},{7,6},{9,8},{10,9},{11,10},{12... | collective-permute-start | bytes 3464 | tf_op jit(solution)/shard_map/ppermute | solution.py:16
  22.3 22.8 %collective-permute-start.8 = (bf16[16,18,2,1]{3,2,1,0:T(2,128)(2,1)S(1)}, bf16[16,18,2,1]{3,2,1,0:T(2,128)(2,1)S(1)}, u32[]{:S(2)}, u32[]{:S(2)}) collective-permute-start(bf16[16,18,2,1]{3,2,1,0:T(2,128)(2,1)S(1)} %get-tuple-element.36), channel_id=1, source_target_pairs={{0,1},{1,2},{2,3},{3,4},{4,5},{5,6},{6,7},{8,9},{9,10},{10,11},{11... | collective-permute-start | bytes 3464 | tf_op jit(solution)/shard_map/ppermute | solution.py:15
  31.3 31.1 %all-to-all-start = ((bf16[8,2,512]{2,1,0:T(2,128)(2,1)}), bf16[8,2,512]{2,1,0:T(2,128)(2,1)S(1)}, u32[]{:S(2)}, u32[]{:S(2)}) async-start(bf16[8,2,512]{2,1,0:T(2,128)(2,1)} %reshape.289), calls=%async_computation | async-start | bytes 32768 | tf_op jit(solution)/shard_map/all_to_all | solution.py:84
  48.5 6.2 copy-start.10
  62.6 32.4 %collective-permute-start.1 = (bf16[16,1,1,512]{3,0,2,1:T(8,128)(2,1)S(1)}, bf16[16,1,1,512]{3,0,2,1:T(8,128)(2,1)S(1)}, u32[]{:S(2)}, u32[]{:S(2)}) collective-permute-start(bf16[16,1,1,512]{3,0,2,1:T(8,128)(2,1)S(1)} %all_to_all.11), channel_id=1, source_target_pairs={{1,0},{2,1},{3,2},{4,3},{5,4},{6,5},{7,6},{8,7},{9,8},{10,9},{11,1... | collective-permute-start | bytes 49160 | tf_op jit(solution)/shard_map/ppermute | solution.py:16
  71.1 23.9 %collective-permute-start = (bf16[16,1,1,512]{3,0,2,1:T(8,128)(2,1)S(1)}, bf16[16,1,1,512]{3,0,2,1:T(8,128)(2,1)}, u32[]{:S(2)}, u32[]{:S(2)}) collective-permute-start(bf16[16,1,1,512]{3,0,2,1:T(8,128)(2,1)S(1)} %all_to_all.11), channel_id=1, source_target_pairs={{0,1},{1,2},{2,3},{3,4},{4,5},{5,6},{6,7},{7,8},{8,9},{9,10},{10,1... | collective-permute-start | bytes 49160 | tf_op jit(solution)/shard_map/ppermute | solution.py:15
  78.6 22.7 %all-to-all-start.2 = ((bf16[8,2,1024]{2,1,0:T(2,128)(2,1)}), bf16[8,2,1024]{2,1,0:T(2,128)(2,1)S(1)}, u32[]{:S(2)}, u32[]{:S(2)}) async-start(bf16[8,2,1024]{2,1,0:T(2,128)(2,1)} %reshape.287), calls=%async_computation.2 | async-start | bytes 65536 | tf_op jit(solution)/shard_map/all_to_all | solution.py:84
  92.2 4.7 copy-start.8
  92.2 4.7 copy-start.9
  101.6 136.7 %collective-permute-start.11 = (bf16[32,1,1,512]{3,0,2,1:T(8,128)(2,1)S(1)}, bf16[32,1,1,512]{3,0,2,1:T(8,128)(2,1)S(1)}, u32[]{:S(2)}, u32[]{:S(2)}) collective-permute-start(bf16[32,1,1,512]{3,0,2,1:T(8,128)(2,1)S(1)} %get-tuple-element.40), channel_id=1, source_target_pairs={{1,0},{2,1},{3,2},{4,3},{5,4},{6,5},{7,6},{8,7},{9,8},{10,9},{11,1... | collective-permute-start | bytes 98312 | tf_op jit(solution)/shard_map/ppermute | solution.py:16
  109.7 128.6 %collective-permute-start.10 = (bf16[32,1,1,512]{3,0,2,1:T(8,128)(2,1)S(1)}, bf16[32,1,1,512]{3,0,2,1:T(8,128)(2,1)S(1)}, u32[]{:S(2)}, u32[]{:S(2)}) collective-permute-start(bf16[32,1,1,512]{3,0,2,1:T(8,128)(2,1)S(1)} %get-tuple-element.40), channel_id=1, source_target_pairs={{0,1},{1,2},{2,3},{3,4},{4,5},{5,6},{6,7},{7,8},{8,9},{9,10},{10,1... | collective-permute-start | bytes 98312 | tf_op jit(solution)/shard_map/ppermute | solution.py:15
  114.7 129.9 %all-to-all-start.1 = ((bf16[8,2,1024]{2,1,0:T(2,128)(2,1)}), bf16[8,2,1024]{2,1,0:T(2,128)(2,1)S(1)}, u32[]{:S(2)}, u32[]{:S(2)}) async-start(bf16[8,2,1024]{2,1,0:T(2,128)(2,1)} %reshape.291), calls=%async_computation.1 | async-start | bytes 65536 | tf_op jit(solution)/shard_map/all_to_all | solution.py:92
  240.7 1.3 copy-start.7
  244.6 12.2 %all-to-all-start.3 = ((bf16[8,2,512]{2,1,0:T(2,128)(2,1)}), bf16[8,2,512]{2,1,0:T(2,128)(2,1)S(1)}, u32[]{:S(2)}, u32[]{:S(2)}) async-start(bf16[8,2,512]{2,1,0:T(2,128)(2,1)} %reshape.293), calls=%async_computation.3 | async-start | bytes 32768 | tf_op jit(solution)/shard_map/all_to_all | solution.py:92
  247.9 382.4 %all-reduce.6.cloned.1.call-start = ((), (), s32[]{:S(2)}) async-start(), calls=%async_computation.4 | async-start | bytes 442368 | tf_op jit(solution)/shard_map/psum | solution.py:116
  248.9 9.2 %collective-permute-start.3 = (bf16[48,1,2,128]{3,0,2,1:T(8,128)(2,1)S(1)}, bf16[48,1,2,128]{3,0,2,1:T(8,128)(2,1)S(1)}, u32[]{:S(2)}, u32[]{:S(2)}) collective-permute-start(bf16[48,1,2,128]{3,0,2,1:T(8,128)(2,1)S(1)} %get-tuple-element.35), channel_id=1, source_target_pairs={{8,0},{16,8},{24,16},{32,24},{40,32},{48,40},{56,48},{64,56},{72,6... | collective-permute-start | bytes 73736 | tf_op jit(solution)/shard_map/ppermute | solution.py:16
  251.8 6.3 collective-permute-start.2
  257.3 10.6 %copy-start.3 = (f32[16,2,1,136,16]{3,4,1,0,2:T(8,128)S(1)}, f32[16,2,1,136,16]{3,4,1,0,2:T(8,128)}, u32[]{:S(2)}) copy-start(f32[16,2,1,136,16]{3,4,1,0,2:T(8,128)} %reshape.252) | copy-start | bytes 835588
  258.3 15.9 %collective-permute-start.5 = (bf16[48,18,2,1]{3,0,2,1:T(8,128)(2,1)S(1)}, bf16[48,18,2,1]{3,0,2,1:T(8,128)(2,1)S(1)}, u32[]{:S(2)}, u32[]{:S(2)}) collective-permute-start(bf16[48,18,2,1]{3,0,2,1:T(8,128)(2,1)S(1)} %get-tuple-element.33), channel_id=1, source_target_pairs={{1,0},{2,1},{3,2},{4,3},{5,4},{6,5},{7,6},{9,8},{10,9},{11,10},{12... | collective-permute-start | bytes 10376 | tf_op jit(solution)/shard_map/ppermute | solution.py:16
  259.6 15.6 %collective-permute-start.4 = (bf16[48,18,2,1]{3,0,2,1:T(8,128)(2,1)S(1)}, bf16[48,18,2,1]{3,0,2,1:T(8,128)(2,1)S(1)}, u32[]{:S(2)}, u32[]{:S(2)}) collective-permute-start(bf16[48,18,2,1]{3,0,2,1:T(8,128)(2,1)S(1)} %get-tuple-element.32), channel_id=1, source_target_pairs={{0,1},{1,2},{2,3},{3,4},{4,5},{5,6},{6,7},{8,9},{9,10},{10,11},{11... | collective-permute-start | bytes 10376 | tf_op jit(solution)/shard_map/ppermute | solution.py:15
  275.2 0.8 copy-start.1
  284.5 9.3 %copy-start.6 = (pred[8,17]{1,0:T(8,128)(4,1)S(1)}, pred[8,17]{1,0:T(8,128)(4,1)}, u32[]{:S(2)}) copy-start(pred[8,17]{1,0:T(8,128)(4,1)} %constant.46) | copy-start | bytes 412
  293.8 1.3 copy-start.2
Sparse Core Ops, SparseCore 0:
  336.4 293.8 all-reduce.5
where the time goes:
time: 648 us; the launch traced here: 639 us
  waiting for transfers between devices  302 us (47%)
  blocking collectives  106 us (16%)
  starting transfers between devices  90.7 us (14%)
  local copies, waits for them, and re-layouts  56.7 us (9%)
  matrix products  50.9 us (8%)
  other arithmetic  18 us (3%)
  between operations  14.9 us (2%)
    psum x1, waiting for transfers between devices, shards(): lax.psum((local_fine, local_coarse), ('wide', 'narrow'))  293 us
    psum x1, blocking collectives, shards(): lax.psum((local_fine, local_coarse), ('wide', 'narrow'))  106 us
    transpose x2, matrix products, weight_grad(): return jnp.transpose(result, (1, 0, 2, 3, 4))  37 us
    ppermute x6, starting transfers between devices, extended_2(): before = lax.ppermute(last, axis, up)  27.7 us
    ppermute x6, starting transfers between devices, extended_2(): after = lax.ppermute(first, axis, down)  27.6 us
    conv_general_dilated x19, local copies, waits for them, and re-layouts, correlate(): lax.conv_general_dilated(padded[None], kernel, (1, 1, 1), 'VALID', dimens...  23.1 us
    all_to_all x2, starting transfers between devices, into_coarse(): lax.all_to_all(shortened(field), 'narrow', split_axis=1, concat_axis=3, t...  20.8 us
    all_to_all x2, starting transfers between devices, into_fine(): lax.all_to_all(shortened(field), 'narrow', split_axis=3, concat_axis=1, t...  14.5 us
  transfers between devices with their start and end apart: 17, of which 4 were waited for; matrix products, arithmetic and copies ran while one was open for 10% of the time, Pallas kernels for 0%

commit v1 on v0

--- a/solution.py
+++ b/solution.py
@@ -113,7 +113,7 @@
     grad_features = (
         grad_joined[:channels] + upsample(into_fine(grad_pooled)).astype(jnp.float32) / 8.0
     ).astype(jnp.bfloat16)
-    fine_total, coarse_total = lax.psum((local_fine, local_coarse), ("wide", "narrow"))
+    fine_total, coarse_total = lax.psum(lax.psum((local_fine, local_coarse), "narrow"), "wide")
     all_cells = (
         features.shape[1]
         * features.shape[2]

time: 648 us -> 1190 us (1.84)
  waiting for transfers between devices: 302 us -> 606 us
  blocking collectives: 106 us -> 330 us
    psum x1 -> x2, waiting for transfers between devices: 293 us -> 602 us  [the longest x1 487 us: shards(): lax.psum(lax.psum((local_fine, local_coarse), 'narrow'), 'wide')]
    psum x1 -> x2, blocking collectives: 106 us -> 330 us  [the longest x1 277 us: shards(): lax.psum(lax.psum((local_fine, local_coarse), 'narrow'), 'wide')]
  transfers between devices with their start and end apart: 17 -> 18, of which waited for: 4 -> 4; matrix products, arithmetic and copies ran while one was open for 10% -> 6% of each run, Pallas kernels for 0% -> 0%
where the time goes in v1:
time: 1190 us; the launch traced here: 1180 us
  waiting for transfers between devices  606 us (51%)
  blocking collectives  330 us (28%)
  starting transfers between devices  95.2 us (8%)
  local copies, waits for them, and re-layouts  58.4 us (5%)
  matrix products  51.6 us (4%)
  other arithmetic  21.1 us (2%)
  between operations  15.1 us (1%)
    psum x1, waiting for transfers between devices, shards(): lax.psum(lax.psum((local_fine, local_coarse), 'narrow'), 'wide')  487 us
    psum x1, blocking collectives, shards(): lax.psum(lax.psum((local_fine, local_coarse), 'narrow'), 'wide')  277 us
    psum x1, waiting for transfers between devices, shards(): lax.psum((local_fine, local_coarse), 'narrow')  115 us
    psum x1, blocking collectives, shards(): lax.psum((local_fine, local_coarse), 'narrow')  53.1 us
    transpose x2, matrix products, weight_grad(): return jnp.transpose(result, (1, 0, 2, 3, 4))  37.7 us
    ppermute x6, starting transfers between devices, extended_2(): after = lax.ppermute(first, axis, down)  33 us
    ppermute x6, starting transfers between devices, extended_2(): before = lax.ppermute(last, axis, up)  26.8 us
  transfers between devices with their start and end apart: 18, of which 4 were waited for; matrix products, arithmetic and copies ran while one was open for 6% of the time, Pallas kernels for 0%

profile of v1, /device:TPU:1, one launch (start us, length us, event | category | flops | bytes accessed | tf_op | source)
XLA Modules:
  0.0 1177.9 jit_solution(5425676697788141247)
XLA Ops:
  7.2 0.8 fusion.97
  8.0 4.6 collective-permute-start.6
  12.6 5.5 collective-permute-start.7
  18.1 1.3 convert_reduce_fusion
  19.7 0.9 reduce_sum.25
  21.0 1.3 collective-permute-start.9
  22.3 8.1 collective-permute-start.8
  31.3 10.0 all-to-all-start
  41.3 3.8 copy.231
  45.1 1.3 fusion.54
  46.7 1.8 reshape.286
  48.6 5.0 copy.219
  53.6 1.0 slice.64
  54.7 5.0 fusion.26
  60.3 2.0 copy.221
  62.6 8.5 collective-permute-start.1
  71.1 2.2 collective-permute-start
  73.3 1.9 slice_reduce_fusion
  75.2 1.8 reduce_sum.37
  76.9 1.0 copy.222
  78.7 10.8 all-to-all-start.2
  89.5 2.8 copy.220
  92.3 2.1 reshape.252
  94.5 0.8 fusion.98
  95.6 0.8 copy.204
  96.4 1.2 fusion.46
  97.6 0.8 fusion.99
  98.7 2.0 copy.233
  101.0 8.2 collective-permute-start.11
  109.2 1.9 collective-permute-start.10
  112.5 2.1 reduce.8
  114.6 1.7 reshape.291
  116.3 11.2 all-to-all-start.1
  127.4 0.9 fusion.74
  128.5 6.4 fusion.101
  134.9 53.1 %psum.30 = f32[32,16,3,3,3]{0,1,4,3,2:T(8,128)S(1)} all-reduce(f32[32,16,3,3,3]{0,1,4,3,2:T(8,128)} %fusion.101), channel_id=1, replica_groups=mesh['wide'=64,'narrow'=8] {'narrow'}, use_global_device_ids=true, to_apply=%region_6.7 | all-reduce | flops 13824 | bytes 110592 | tf_op jit(solution)/shard_map/psum | solution.py:116
  188.0 277.0 %psum.31 = f32[32,16,3,3,3]{0,1,4,3,2:T(8,128)S(1)} all-reduce(f32[32,16,3,3,3]{0,1,4,3,2:T(8,128)S(1)} %psum.30), channel_id=1, replica_groups=mesh['wide'=64,'narrow'=8] {'wide'}, use_global_device_ids=true, to_apply=%region_7.8 | all-reduce | flops 13824 | bytes 110592 | tf_op jit(solution)/shard_map/psum | solution.py:116
  465.7 0.9 fusion.55
  467.2 1.7 copy.225
  468.9 1.1 fusion.33
  470.5 1.4 reduce.9
  471.9 0.8 reshape.293
  472.7 3.3 all-to-all-start.3
  476.1 0.9 reshape.292
  477.7 8.3 collective-permute-start.3
  486.0 1.9 collective-permute-start.2
  489.4 1.3 collective-permute-start.5
  490.7 8.1 collective-permute-start.4
  498.8 0.8 copy.236
  499.5 2.9 collective-permute-done.5
  502.5 1.5 collective-permute-done.4
  504.0 0.8 copy-done.2
  504.7 2.0 fusion.111
  506.7 4.9 copy.240
  511.6 1.3 pad.22.clone
  513.3 6.5 fusion.9
  519.8 2.7 copy.214
  522.6 2.1 fusion.110
  524.7 8.8 copy.230
  533.6 31.3 %fusion.100 = f32[16,48,3,3,3]{1,0,4,3,2:T(8,128)} fusion(bf16[48,1,18,4,130]{0,1,4,3,2:T(2,128)(2,1)} %copy.230, bf16[16,1,16,2,128]{0,1,4,3,2:T(2,128)(2,1)} %copy.231), kind=kOutput, calls=%fused_computation.139 | convolution fusion | flops 169869312 | bytes 1112576 | tf_op jit(solution)/shard_map/transpose | solution.py:46
  566.3 114.6 %all-reduce.7.cloned.1.call-done = f32[16,48,3,3,3]{1,0,4,3,2:T(8,128)} async-done(((f32[16,48,3,3,3]{1,0,4,3,2:T(8,128)}), f32[16,48,3,3,3]{1,0,4,3,2:T(8,128)}) %all-reduce.7.cloned.1.call-update) | async-done | bytes 82960 | tf_op jit(solution)/shard_map/psum | solution.py:116
  680.9 0.8 copy.235
  681.7 487.3 %all-reduce.9.cloned.1.call-done = f32[16,48,3,3,3]{1,0,4,3,2:T(8,128)} async-done(((f32[16,48,3,3,3]{1,0,4,3,2:T(8,128)}), f32[16,48,3,3,3]{1,0,4,3,2:T(8,128)}) %all-reduce.9.cloned.1.call-update) | async-done | bytes 82960 | tf_op jit(solution)/shard_map/psum | solution.py:116
  1169.0 1.6 broadcast_multiply_fusion.1
  (95 shorter events, 11.7 us)
Async XLA Ops:
  7.2 47.5 %copy-start = (bf16[16,48,3,3,3]{1,0,4,3,2:T(8,128)(2,1)S(1)}, bf16[16,48,3,3,3]{1,0,4,3,2:T(8,128)(2,1)}, u32[]{:S(2)}) copy-start(bf16[16,48,3,3,3]{1,0,4,3,2:T(8,128)(2,1)} %param.7) | copy-start | bytes 124420
  7.2 13.4 %copy-start.3 = (bf16[16,16,2,128]{3,2,1,0:T(2,128)(2,1)S(1)}, bf16[16,16,2,128]{3,2,1,0:T(2,128)(2,1)}, u32[]{:S(2)}) copy-start(bf16[16,16,2,128]{3,2,1,0:T(2,128)(2,1)} %param.5) | copy-start | bytes 393220
  7.2 34.1 %copy-start.4 = (bf16[16,16,2,128]{3,2,1,0:T(2,128)(2,1)S(1)}, bf16[16,16,2,128]{3,2,1,0:T(2,128)(2,1)}, u32[]{:S(2)}) copy-start(bf16[16,16,2,128]{3,2,1,0:T(2,128)(2,1)} %param.4) | copy-start | bytes 393220
  8.0 12.6 %collective-permute-start.6 = (bf16[16,1,2,128]{3,2,1,0:T(2,128)(2,1)S(1)}, bf16[16,1,2,128]{3,2,1,0:T(2,128)(2,1)S(1)}, u32[]{:S(2)}, u32[]{:S(2)}) collective-permute-start(bf16[16,1,2,128]{3,2,1,0:T(2,128)(2,1)S(1)} %get-tuple-element.39), channel_id=1, source_target_pairs={{0,8},{8,16},{16,24},{24,32},{32,40},{40,48},{48,56},{56,64},{64,7... | collective-permute-start | bytes 24584 | tf_op jit(solution)/shard_map/ppermute | solution.py:15
  12.6 8.1 collective-permute-start.7
  21.0 24.1 %collective-permute-start.9 = (bf16[16,18,2,1]{3,2,1,0:T(2,128)(2,1)S(1)}, bf16[16,18,2,1]{3,2,1,0:T(2,128)(2,1)S(1)}, u32[]{:S(2)}, u32[]{:S(2)}) collective-permute-start(bf16[16,18,2,1]{3,2,1,0:T(2,128)(2,1)S(1)} %get-tuple-element.37), channel_id=1, source_target_pairs={{1,0},{2,1},{3,2},{4,3},{5,4},{6,5},{7,6},{9,8},{10,9},{11,10},{12... | collective-permute-start | bytes 3464 | tf_op jit(solution)/shard_map/ppermute | solution.py:16
  22.3 22.8 %collective-permute-start.8 = (bf16[16,18,2,1]{3,2,1,0:T(2,128)(2,1)S(1)}, bf16[16,18,2,1]{3,2,1,0:T(2,128)(2,1)S(1)}, u32[]{:S(2)}, u32[]{:S(2)}) collective-permute-start(bf16[16,18,2,1]{3,2,1,0:T(2,128)(2,1)S(1)} %get-tuple-element.36), channel_id=1, source_target_pairs={{0,1},{1,2},{2,3},{3,4},{4,5},{5,6},{6,7},{8,9},{9,10},{10,11},{11... | collective-permute-start | bytes 3464 | tf_op jit(solution)/shard_map/ppermute | solution.py:15
  31.3 31.1 %all-to-all-start = ((bf16[8,2,512]{2,1,0:T(2,128)(2,1)}), bf16[8,2,512]{2,1,0:T(2,128)(2,1)S(1)}, u32[]{:S(2)}, u32[]{:S(2)}) async-start(bf16[8,2,512]{2,1,0:T(2,128)(2,1)} %reshape.289), calls=%async_computation | async-start | bytes 32768 | tf_op jit(solution)/shard_map/all_to_all | solution.py:84
  48.5 6.1 copy-start.10
  62.6 31.9 %collective-permute-start.1 = (bf16[16,1,1,512]{3,0,2,1:T(8,128)(2,1)S(1)}, bf16[16,1,1,512]{3,0,2,1:T(8,128)(2,1)S(1)}, u32[]{:S(2)}, u32[]{:S(2)}) collective-permute-start(bf16[16,1,1,512]{3,0,2,1:T(8,128)(2,1)S(1)} %all_to_all.11), channel_id=1, source_target_pairs={{1,0},{2,1},{3,2},{4,3},{5,4},{6,5},{7,6},{8,7},{9,8},{10,9},{11,1... | collective-permute-start | bytes 49160 | tf_op jit(solution)/shard_map/ppermute | solution.py:16
  71.1 23.4 %collective-permute-start = (bf16[16,1,1,512]{3,0,2,1:T(8,128)(2,1)S(1)}, bf16[16,1,1,512]{3,0,2,1:T(8,128)(2,1)}, u32[]{:S(2)}, u32[]{:S(2)}) collective-permute-start(bf16[16,1,1,512]{3,0,2,1:T(8,128)(2,1)S(1)} %all_to_all.11), channel_id=1, source_target_pairs={{0,1},{1,2},{2,3},{3,4},{4,5},{5,6},{6,7},{7,8},{8,9},{9,10},{10,1... | collective-permute-start | bytes 49160 | tf_op jit(solution)/shard_map/ppermute | solution.py:15
  78.7 22.1 %all-to-all-start.2 = ((bf16[8,2,1024]{2,1,0:T(2,128)(2,1)}), bf16[8,2,1024]{2,1,0:T(2,128)(2,1)S(1)}, u32[]{:S(2)}, u32[]{:S(2)}) async-start(bf16[8,2,1024]{2,1,0:T(2,128)(2,1)} %reshape.287), calls=%async_computation.2 | async-start | bytes 65536 | tf_op jit(solution)/shard_map/all_to_all | solution.py:84
  92.3 4.1 copy-start.7
  92.3 4.1 copy-start.9
  101.0 364.6 %collective-permute-start.11 = (bf16[32,1,1,512]{3,0,2,1:T(8,128)(2,1)S(1)}, bf16[32,1,1,512]{3,0,2,1:T(8,128)(2,1)}, u32[]{:S(2)}, u32[]{:S(2)}) collective-permute-start(bf16[32,1,1,512]{3,0,2,1:T(8,128)(2,1)S(1)} %get-tuple-element.40), channel_id=1, source_target_pairs={{1,0},{2,1},{3,2},{4,3},{5,4},{6,5},{7,6},{8,7},{9,8},{10,9},{11,1... | collective-permute-start | bytes 98312 | tf_op jit(solution)/shard_map/ppermute | solution.py:16
  109.2 356.5 %collective-permute-start.10 = (bf16[32,1,1,512]{3,0,2,1:T(8,128)(2,1)S(1)}, bf16[32,1,1,512]{3,0,2,1:T(8,128)(2,1)}, u32[]{:S(2)}, u32[]{:S(2)}) collective-permute-start(bf16[32,1,1,512]{3,0,2,1:T(8,128)(2,1)S(1)} %get-tuple-element.40), channel_id=1, source_target_pairs={{0,1},{1,2},{2,3},{3,4},{4,5},{5,6},{6,7},{7,8},{8,9},{9,10},{10,1... | collective-permute-start | bytes 98312 | tf_op jit(solution)/shard_map/ppermute | solution.py:15
  116.3 356.4 %all-to-all-start.1 = ((bf16[8,2,1024]{2,1,0:T(2,128)(2,1)}), bf16[8,2,1024]{2,1,0:T(2,128)(2,1)}, u32[]{:S(2)}, u32[]{:S(2)}) async-start(bf16[8,2,1024]{2,1,0:T(2,128)(2,1)} %reshape.291), calls=%async_computation.1 | async-start | bytes 65536 | tf_op jit(solution)/shard_map/all_to_all | solution.py:92
  188.0 280.9 %copy-start.8 = (bf16[32,16,3,3,3]{0,1,4,3,2:T(8,128)(2,1)S(1)}, bf16[32,16,3,3,3]{0,1,4,3,2:T(8,128)(2,1)}, u32[]{:S(2)}) copy-start(bf16[32,16,3,3,3]{0,1,4,3,2:T(8,128)(2,1)} %param.6) | copy-start | bytes 82948
  468.9 1.3 copy-start.6
  472.7 15.3 %all-to-all-start.3 = ((bf16[8,2,512]{2,1,0:T(2,128)(2,1)}), bf16[8,2,512]{2,1,0:T(2,128)(2,1)S(1)}, u32[]{:S(2)}, u32[]{:S(2)}) async-start(bf16[8,2,512]{2,1,0:T(2,128)(2,1)} %reshape.293), calls=%async_computation.3 | async-start | bytes 32768 | tf_op jit(solution)/shard_map/all_to_all | solution.py:92
  476.0 204.9 %all-reduce.7.cloned.1.call-start = ((), (), s32[]{:S(2)}) async-start(), calls=%async_computation.4 | async-start | bytes 442368 | tf_op jit(solution)/shard_map/psum | solution.py:116
  477.7 11.4 collective-permute-start.3
  486.0 3.2 collective-permute-start.2
  489.4 13.1 %collective-permute-start.5 = (bf16[48,18,2,1]{3,0,2,1:T(8,128)(2,1)S(1)}, bf16[48,18,2,1]{3,0,2,1:T(8,128)(2,1)S(1)}, u32[]{:S(2)}, u32[]{:S(2)}) collective-permute-start(bf16[48,18,2,1]{3,0,2,1:T(8,128)(2,1)S(1)} %get-tuple-element.33), channel_id=1, source_target_pairs={{1,0},{2,1},{3,2},{4,3},{5,4},{6,5},{7,6},{9,8},{10,9},{11,10},{12... | collective-permute-start | bytes 10376 | tf_op jit(solution)/shard_map/ppermute | solution.py:16
  490.7 13.3 %collective-permute-start.4 = (bf16[48,18,2,1]{3,0,2,1:T(8,128)(2,1)S(1)}, bf16[48,18,2,1]{3,0,2,1:T(8,128)(2,1)S(1)}, u32[]{:S(2)}, u32[]{:S(2)}) collective-permute-start(bf16[48,18,2,1]{3,0,2,1:T(8,128)(2,1)S(1)} %get-tuple-element.32), channel_id=1, source_target_pairs={{0,1},{1,2},{2,3},{3,4},{4,5},{5,6},{6,7},{8,9},{9,10},{10,11},{11... | collective-permute-start | bytes 10376 | tf_op jit(solution)/shard_map/ppermute | solution.py:15
  502.5 1.5 copy-start.1
  504.0 0.8 copy-start.2
  533.5 31.4 %copy-start.5 = (pred[8,17]{1,0:T(8,128)(4,1)S(1)}, pred[8,17]{1,0:T(8,128)(4,1)}, u32[]{:S(2)}) copy-start(pred[8,17]{1,0:T(8,128)(4,1)} %constant.46) | copy-start | bytes 412
  564.9 604.1 %all-reduce.9.cloned.1.call-start = ((), (), s32[]{:S(2)}) async-start(), calls=%async_computation.5 | async-start | bytes 442368 | tf_op jit(solution)/shard_map/psum | solution.py:116
Sparse Core Ops, SparseCore 0:
  565.0 115.7 all-reduce.6
  684.0 484.9 all-reduce.8
